TPU v7x, 32 devices: a whole 2x2x4 slice. The times are simulated.
32 devices in a mesh: aux: 4 (over y, x), orb: 8 (over z, core).
Axes of the slice: x: 2, y: 2, z: 4, core: 2. Of those that a mesh axis runs over, the one named last changes fastest.
Arguments:
- integrals: bfloat16 [4096, 4, 2048], P('aux'), may hold values from -6 to 6
- int_pattern: int32 [64, 32], P('aux'), may hold values 0 or 1
- density: bfloat16 [2, 2048, 2048], P(None, 'aux', 'orb'), may hold values from -0.125 to 0.125
- dens_pattern: int32 [32, 32], P('aux', 'orb'), may hold values 0 or 1
- virt_ints: bfloat16 [2, 4096, 4, 2048], P(None, 'aux', None, 'orb'), may hold values from -0.0625 to 0.0625
Outputs:
- chi: float32 [2, 4096, 4096], P(None, 'orb', 'aux')
All inputs are finite; a program needn't handle non-finite values.
Results may differ from a plain program's by a relative error of at most 0.012.
Values may be sent and summed in bfloat16 or wider, within the bound.
A program may use at most 128 MiB of HBM per device.

v0:
```python
import jax
import jax.numpy as jnp
from jax import lax
from jax.sharding import PartitionSpec as P

BLK = 64


def expand(pattern, block_width):
    return jnp.repeat(jnp.repeat(pattern, block_width, axis=0), block_width, axis=1).astype(
        jnp.bfloat16
    )


def on_device(integrals, int_pattern, density, dens_pattern, virt_ints):
    aux_rows, slab_width, orbitals = integrals.shape
    times_count, _, columns = density.shape
    int_mask = expand(int_pattern, BLK)
    integral_rows = (integrals * int_mask[:, None, :]).reshape(aux_rows * slab_width, orbitals)
    masked_density = density * expand(dens_pattern, BLK)[None]
    occupied_list = []
    for moment in range(times_count):
        occupied_list.append(
            jnp.dot(
                integral_rows,
                lax.all_gather(masked_density[moment], "aux", axis=0, tiled=True),
                preferred_element_type=jnp.float32,
            )
        )
    occupied = jnp.stack(occupied_list)
    occupied = occupied.astype(jnp.bfloat16).reshape(times_count, aux_rows, slab_width * columns)
    virtual_rows = virt_ints.reshape(times_count, virt_ints.shape[1], slab_width * columns)
    partial_chi = jnp.einsum(
        "tpk,tqk->tpq",
        lax.all_gather(occupied, "aux", axis=1, tiled=True),
        virtual_rows,
        preferred_element_type=jnp.float32,
    )
    return lax.psum_scatter(
        partial_chi.astype(jnp.bfloat16), "orb", scatter_dimension=1, tiled=True
    ).astype(jnp.float32)


def solution(mesh):
    in_specs = (
        P("aux", None, None),
        P("aux", None),
        P(None, "aux", "orb"),
        P("aux", "orb"),
        P(None, "aux", None, "orb"),
    )
    out_specs = P(None, "orb", "aux")
    return jax.shard_map(
        on_device, mesh=mesh, in_specs=in_specs, out_specs=out_specs, check_vma=False
    )
```

profile of v0, /device:TPU:0, one launch (start us, length us, event | category | flops | bytes accessed | tf_op | source)
XLA Modules:
  0.0 456.4 jit_solution(6591033319536357993)
XLA Ops:
  6.5 0.7 convert_element_type.41
  7.3 0.1 convert_element_type.42
  7.4 0.1 copy.9
  7.6 1.1 broadcast_multiply_fusion.1
  8.7 0.8 fusion.2
  9.6 0.7 all-gather.8.cloned.1.call-update
  10.3 0.7 convert_element_type.38
  11.1 0.1 broadcast_in_dim.14
  11.3 0.1 convert_element_type.39
  11.4 2.6 broadcast_in_dim.15
  13.9 6.6 %copy.8 = bf16[1024,2048]{1,0:T(8,128)(2,1)} copy(bf16[1024,2048]{0,1:T(8,128)(2,1)} %bitcast.16) | data formatting | bytes 8388608 | tf_op jit(solution)/shard_map/convert_element_type | solution.py:10
  20.5 13.4 %broadcast_multiply_fusion = bf16[1024,4,2048]{2,1,0:T(4,128)(2,1)} fusion(bf16[1024,4,2048]{2,1,0:T(4,128)(2,1)} %param.5, bf16[1024,2048]{1,0:T(8,128)(2,1)} %copy.8), kind=kLoop, calls=%fused_computation.1 | loop fusion | flops 8388608 | bytes 37748736 | tf_op jit(solution)/shard_map/mul | solution.py:19
  34.0 23.6 %reshape.31 = bf16[4096,2048]{1,0:T(8,128)(2,1)} reshape(bf16[1024,4,2048]{2,1,0:T(4,128)(2,1)} %broadcast_multiply_fusion) | data formatting | bytes 33554432 | tf_op jit(solution)/shard_map/reshape | solution.py:19
  57.6 12.0 %convolution_convert_fusion.1 = bf16[4096,256]{1,0:T(8,128)(2,1)} fusion(bf16[4096,2048]{1,0:T(8,128)(2,1)} %reshape.31, bf16[1,2048,256]{2,1,0:T(8,128)(2,1)} %all-gather.10.cloned.1.call-done), kind=kOutput, calls=%fused_computation.2 | convolution fusion | flops 4296015872 | bytes 19922944 | tf_op jit(solution)/shard_map/dot_general | solution.py:24
  69.6 3.1 stack.10
  72.7 11.9 %convolution_convert_fusion.2 = bf16[4096,256]{1,0:T(8,128)(2,1)} fusion(bf16[4096,2048]{1,0:T(8,128)(2,1)} %reshape.31, bf16[1,2048,256]{2,1,0:T(8,128)(2,1)} %all-gather.8.cloned.1.call-done), kind=kOutput, calls=%fused_computation.3 | convolution fusion | flops 4296015872 | bytes 19922944 | tf_op jit(solution)/shard_map/dot_general | solution.py:24
  84.6 4.3 stack.9
  88.9 4.0 pad_maximum_fusion
  93.0 0.2 reduce-scatter.2.cloned.1.call-start
  93.2 7.7 %reshape.32 = bf16[2,1024,1024]{2,1,0:T(8,128)(2,1)} reshape(bf16[2,1024,4,256]{3,2,1,0:T(4,128)(2,1)} %param.9) | data formatting | bytes 8388608 | tf_op jit(solution)/shard_map/reshape | solution.py:32
  100.9 152.2 %all-gather.6.cloned.1.call-done = bf16[2,4096,1024]{2,1,0:T(8,128)(2,1)} async-done(((bf16[2,1024,1024]{2,1,0:T(8,128)(2,1)}), bf16[2,4096,1024]{2,1,0:T(8,128)(2,1)}) %all-gather.6.cloned.1.call-update) | async-done | bytes 16777232 | tf_op jit(solution)/shard_map/all_gather | solution.py:35
  253.1 24.3 %convolution_convert_fusion = bf16[2,4096,1024]{2,1,0:T(8,128)(2,1)} fusion(bf16[2,4096,1024]{2,1,0:T(8,128)(2,1)} %all-gather.6.cloned.1.call-done, bf16[2,1024,1024]{2,1,0:T(8,128)(2,1)} %reshape.32), kind=kOutput, calls=%fused_computation | convolution fusion | flops 17188257792 | bytes 37748736 | tf_op jit(solution)/shard_map/tpk,tqk->tpq/dot_general | solution.py:33
  277.4 168.4 %reduce-scatter.2.cloned.1.call-done = bf16[2,512,1024]{2,1,0:T(8,128)(2,1)} async-done(((bf16[2,4096,1024]{2,1,0:T(8,128)(2,1)}), bf16[2,512,1024]{2,1,0:T(8,128)(2,1)}) %reduce-scatter.2.cloned.1.call-update) | async-done | bytes 2097168 | tf_op jit(solution)/shard_map/reduce_scatter | solution.py:39
  445.8 4.1 convert_element_type.45
  (11 shorter events, 0.3 us)
Async XLA Ops:
  6.5 51.0 %all-gather.10.cloned.1.call-start = ((), (), s32[]{:S(2)}) async-start(), calls=%async_computation.4 | async-start | bytes 1310720 | tf_op jit(solution)/shard_map/all_gather | solution.py:26
  9.5 63.2 %all-gather.8.cloned.1.call-start = ((), (), s32[]{:S(2)}) async-start(), calls=%async_computation.3 | async-start | bytes 1310720 | tf_op jit(solution)/shard_map/all_gather | solution.py:26
  10.3 242.8 %all-gather.6.cloned.1.call-start = ((), (), s32[]{:S(2)}) async-start(), calls=%async_computation.1 | async-start | bytes 20971520 | tf_op jit(solution)/shard_map/all_gather | solution.py:35
  93.0 352.9 %reduce-scatter.2.cloned.1.call-start = ((), (), s32[]{:S(2)}) async-start(), calls=%async_computation.2 | async-start | bytes 18874368 | tf_op jit(solution)/shard_map/reduce_scatter | solution.py:39
Sparse Core Ops, SparseCore 0:
  9.6 29.3 all-gather.9
  40.8 26.6 all-gather.7
  93.1 159.9 all-gather.5
  277.6 168.2 reduce-scatter.1
where the time goes:
time: 458 us; the launch traced here: 456 us
  waiting for transfers between devices  321 us (70%)
  local copies, waits for them, and re-layouts  49.4 us (11%)
  matrix products  48.2 us (11%)
  other arithmetic  24 us (5%)
  between operations  13.2 us (3%)
    reduce_scatter x1, waiting for transfers between devices, on_device(): lax.psum_scatter(partial_chi.astype(jnp.bfloat16), 'orb', scatter_dimensi...  168 us
    all_gather x1, waiting for transfers between devices, on_device(): lax.all_gather(occupied, 'aux', axis=1, tiled=True)  152 us
    dot_general x1, matrix products, on_device(): jnp.einsum('tpk,tqk->tpq', lax.all_gather(occupied, 'aux', axis=1, tiled=...  24.3 us
    dot_general x2, matrix products, on_device(): jnp.dot(integral_rows, lax.all_gather(masked_density[moment], 'aux', axis...  23.9 us
    reshape x1, local copies, waits for them, and re-layouts, on_device(): (integrals * int_mask[:, None, :]).reshape(aux_rows * slab_width, orbitals)  23.6 us
    mul x1, other arithmetic, on_device(): integrals * int_mask[:, None, :]  13.4 us
  transfers between devices with their start and end apart: 4, of which 2 were waited for; matrix products, arithmetic and copies ran while one was open for 15% of the time, Pallas kernels for 0%

commit v1 on v0

--- a/solution.py
+++ b/solution.py
@@ -1,15 +1,250 @@
+import functools
+
 import jax
 import jax.numpy as jnp
 from jax import lax
+from jax.experimental import pallas as pl
+from jax.experimental.pallas import tpu as pltpu
 from jax.sharding import PartitionSpec as P
 
 BLK = 64
+CHUNKS = 16
+MESH = pl.DeviceIdType.MESH
 
 
 def expand(pattern, block_width):
     return jnp.repeat(jnp.repeat(pattern, block_width, axis=0), block_width, axis=1).astype(
         jnp.bfloat16
     )
+
+
+def ring_kernel(chunks, ints, d_own, d_sib, v_own, v_sib, out, occ, psum, zrecv, ibuf, isem, xs, xr, zs, zr):
+    slab, rows = ibuf.shape[1], ibuf.shape[2]
+    per_moment = out.shape[1] // rows
+    cols = d_own.shape[2]
+    width = slab * cols
+    half = rows // 2
+    a = lax.axis_index("aux")
+    o = lax.axis_index("orb")
+    z = o // 2
+    ax = a + 1 - 2 * (a % 2)
+    ay = (a + 2) % 4
+    ad = 3 - a
+
+    def rcopy(src, dst, send, recv, dev):
+        return pltpu.make_async_remote_copy(
+            src_ref=src, dst_ref=dst, send_sem=send, recv_sem=recv, device_id=dev, device_id_type=MESH
+        )
+
+    def own(i, kind, slot):
+        ref = occ.at[slot, i]
+        return rcopy(ref, ref, xs.at[kind, i], xr.at[kind, i], (ax if kind == 0 else ay, o))
+
+    def forward(i, kind, slot):
+        ref = occ.at[slot, i, pl.ds(0 if kind == 2 else half, half)]
+        return rcopy(ref, ref, xs.at[kind, i], xr.at[kind, i], (ay if kind == 2 else ax, o))
+
+    def up(i, frm, at_end):
+        low = frm + 1
+        src = psum.at[i, pl.ds(low, 4 - low)] if at_end else zrecv.at[i, pl.ds(low + 1, 4 - low)]
+        return rcopy(src, zrecv.at[i, pl.ds(low + 1, 4 - low)], zs.at[0, i], zr.at[0, i], (a, 2 * (frm + 1) + o % 2))
+
+    def down(i, frm, at_end):
+        src = psum.at[i, pl.ds(0, frm)] if at_end else zrecv.at[i, pl.ds(0, frm)]
+        return rcopy(src, zrecv.at[i, pl.ds(0, frm)], zs.at[1, i], zr.at[1, i], (a, 2 * (frm - 1) + o % 2))
+
+    def fetch(i):
+        return pltpu.make_async_copy(
+            ints.at[:, pl.ds((i % per_moment) * rows, rows), :], ibuf.at[i % 2], isem.at[i % 2]
+        )
+
+    fetch(0).start()
+
+    barrier = pltpu.get_barrier_semaphore()
+    pl.semaphore_signal(barrier, inc=1, device_id=(ax, o), device_id_type=MESH)
+    pl.semaphore_signal(barrier, inc=1, device_id=(ay, o), device_id_type=MESH)
+
+    @pl.when(z > 0)
+    def _():
+        pl.semaphore_signal(barrier, inc=1, device_id=(a, o - 2), device_id_type=MESH)
+
+    @pl.when(z < 3)
+    def _():
+        pl.semaphore_signal(barrier, inc=1, device_id=(a, o + 2), device_id_type=MESH)
+
+    inner = (z > 0) & (z < 3)
+
+    @pl.when(inner)
+    def _():
+        pl.semaphore_wait(barrier, 4)
+
+    @pl.when(jnp.logical_not(inner))
+    def _():
+        pl.semaphore_wait(barrier, 3)
+
+    def make(i):
+        fetch(i).wait()
+
+        @pl.when(i + 1 < chunks)
+        def _():
+            fetch(i + 1).start()
+
+        t = i // per_moment
+        x = ibuf[i % 2].reshape(slab * rows, ibuf.shape[3])
+        for base, dens in ((0, d_own), (width, d_sib)):
+            y = jnp.dot(x, dens[t], preferred_element_type=jnp.float32).astype(jnp.bfloat16)
+            for s in range(slab):
+                occ[a, i, :, base + s * cols : base + (s + 1) * cols] = y[s * rows : (s + 1) * rows]
+        own(i, 0, a).start()
+        own(i, 1, a).start()
+
+    def relay(i):
+        own(i, 0, ax).wait_recv()
+        forward(i, 2, ax).start()
+        own(i, 1, ay).wait_recv()
+        forward(i, 3, ay).start()
+
+    def multiply(i):
+        forward(i, 2, ad).wait_recv()
+        forward(i, 3, ad).wait_recv()
+        t = i // per_moment
+        for d in range(0, 4, 2):
+            left = occ[d : d + 2, i].reshape(2 * rows, 2 * width)
+            p = jnp.dot(left[:, :width], v_own[t], preferred_element_type=jnp.float32)
+            p += jnp.dot(left[:, width:], v_sib[t], preferred_element_type=jnp.float32)
+            psum[i, d : d + 2] = p.astype(jnp.bfloat16).reshape(2, rows, psum.shape[3])
+
+        @pl.when(z == 0)
+        def _():
+            up(i, 0, True).start()
+
+        @pl.when(z == 3)
+        def _():
+            down(i, 3, True).start()
+
+    def add(i, slot, d):
+        total = zrecv[i, slot].astype(jnp.float32) + psum[i, d].astype(jnp.float32)
+        zrecv[i, slot] = total.astype(jnp.bfloat16)
+
+    def hop1(i):
+        @pl.when(z == 1)
+        def _():
+            up(i, 0, True).wait_recv()
+            for d in (2, 3):
+                add(i, d + 1, d)
+            up(i, 1, False).start()
+
+        @pl.when(z == 2)
+        def _():
+            down(i, 3, True).wait_recv()
+            for d in (0, 1):
+                add(i, d, d)
+            down(i, 2, False).start()
+
+    def hop2(i):
+        @pl.when(z == 2)
+        def _():
+            up(i, 1, False).wait_recv()
+            add(i, 4, 3)
+            up(i, 2, False).start()
+
+        @pl.when(z == 1)
+        def _():
+            down(i, 2, False).wait_recv()
+            add(i, 0, 0)
+            down(i, 1, False).start()
+
+    def finish(i):
+        where = pl.ds((i % per_moment) * rows, rows)
+        t = i // per_moment
+
+        @pl.when(z == 0)
+        def _():
+            down(i, 1, False).wait_recv()
+            out[t, where] = psum[i, 0].astype(jnp.float32) + zrecv[i, 0].astype(jnp.float32)
+
+        @pl.when(z == 3)
+        def _():
+            up(i, 2, False).wait_recv()
+            out[t, where] = psum[i, 3].astype(jnp.float32) + zrecv[i, 4].astype(jnp.float32)
+
+        @pl.when(inner)
+        def _():
+            total = zrecv[i, z].astype(jnp.float32) + zrecv[i, z + 1].astype(jnp.float32)
+            out[t, where] = total + psum[i, z].astype(jnp.float32)
+
+    stages = ((make, 0), (relay, 2), (multiply, 3), (hop1, 4), (hop2, 5), (finish, 6))
+
+    @pl.loop(0, chunks + stages[-1][1])
+    def _(step):
+        for stage, lag in stages:
+
+            @pl.when((step >= lag) & (step < chunks + lag))
+            def _(stage=stage, lag=lag):
+                stage(step - lag)
+
+    @pl.loop(0, chunks)
+    def _(i):
+        own(i, 0, a).wait_send()
+        own(i, 1, a).wait_send()
+        forward(i, 2, ax).wait_send()
+        forward(i, 3, ay).wait_send()
+        for place in range(4):
+
+            @pl.when(z == place)
+            def _(place=place):
+                if place < 3:
+                    up(i, place, place == 0).wait_send()
+                if place > 0:
+                    down(i, place, place == 3).wait_send()
+
+
+def on_grid(integrals, int_pattern, density, dens_pattern, virt_ints):
+    aux_rows, slab, orbitals = integrals.shape
+    times, _, cols = density.shape
+    core = lax.axis_index("orb") % 2
+    mine = aux_rows // 2
+    pairs = [(i, i + 1 - 2 * (i % 2)) for i in range(8)]
+    v_other = lax.ppermute(virt_ints, "orb", pairs)
+    masked_density = density * expand(dens_pattern, BLK)[None]
+    d_own = lax.all_gather(masked_density, "aux", axis=1, tiled=True)
+    d_sib = lax.ppermute(d_own, "orb", pairs)
+    picked = lax.dynamic_slice_in_dim(integrals, core * mine, mine, 0)
+    pattern = lax.dynamic_slice_in_dim(int_pattern, core * (mine // BLK), mine // BLK, 0)
+    ints = jnp.transpose(picked * expand(pattern, BLK)[:, None, :], (1, 0, 2))
+
+    def turned(v):
+        return jnp.transpose(v, (0, 2, 3, 1)).reshape(times, slab * cols, aux_rows)
+
+    rows = times * mine // CHUNKS
+    width = slab * cols
+    bf16 = jnp.bfloat16
+    vmem = pl.BlockSpec(memory_space=pltpu.VMEM)
+    return pl.pallas_call(
+        functools.partial(ring_kernel, CHUNKS),
+        out_shape=jax.ShapeDtypeStruct((times, mine, aux_rows), jnp.float32),
+        in_specs=[pl.BlockSpec(memory_space=pl.ANY), vmem, vmem, vmem, vmem],
+        out_specs=vmem,
+        scratch_shapes=[
+            pltpu.VMEM((4, CHUNKS, rows, 2 * width), bf16),
+            pltpu.VMEM((CHUNKS, 4, rows, aux_rows), bf16),
+            pltpu.VMEM((CHUNKS, 5, rows, aux_rows), bf16),
+            pltpu.VMEM((2, slab, rows, orbitals), bf16),
+            pltpu.SemaphoreType.DMA((2,)),
+            pltpu.SemaphoreType.DMA((4, CHUNKS)),
+            pltpu.SemaphoreType.DMA((4, CHUNKS)),
+            pltpu.SemaphoreType.DMA((2, CHUNKS)),
+            pltpu.SemaphoreType.DMA((2, CHUNKS)),
+        ],
+        compiler_params=pltpu.CompilerParams(
+            collective_id=0, has_side_effects=True, vmem_limit_bytes=60 * 1024 * 1024
+        ),
+        cost_estimate=pl.CostEstimate(
+            flops=2 * times * slab * aux_rows * cols * (orbitals + 4 * aux_rows),
+            bytes_accessed=64 << 20,
+            transcendentals=0,
+        ),
+    )(ints, d_own, d_sib, turned(virt_ints), turned(v_other))
 
 
 def on_device(integrals, int_pattern, density, dens_pattern, virt_ints):
@@ -50,6 +285,11 @@
         P(None, "aux", None, "orb"),
     )
     out_specs = P(None, "orb", "aux")
+    small = mesh.shape["aux"] == 4 and mesh.shape["orb"] == 8
     return jax.shard_map(
-        on_device, mesh=mesh, in_specs=in_specs, out_specs=out_specs, check_vma=False
-    )
+        on_grid if small else on_device,
+        mesh=mesh,
+        in_specs=in_specs,
+        out_specs=out_specs,
+        check_vma=False,
+    )

time: 458 us -> 288 us (0.63)
  waiting for transfers between devices: 321 us -> 37.7 us
  Pallas kernels: 0 us -> 183 us
  matrix products: 48.2 us -> 0 us
  local copies, waits for them, and re-layouts: 49.4 us -> 33.2 us
  other arithmetic: 24 us -> 19.1 us
    pallas_call x0 -> x1, Pallas kernels: none -> 183 us  [on_grid(): pl.pallas_call(functools.partial(ring_kernel, CHUNKS), out_shape=jax.Shap...]
    reduce_scatter x1 -> x0, waiting for transfers between devices: 168 us -> none  [on_device(): lax.psum_scatter(partial_chi.astype(jnp.bfloat16), 'orb', scatter_dimensi...]
    all_gather x3 -> x1, waiting for transfers between devices: 152 us -> 37.6 us  [on_grid(): d_own = lax.all_gather(masked_density, 'aux', axis=1, tiled=True)]
    dot_general x3 -> x0, matrix products: 48.2 us -> none  [the longest x1 24.3 us: on_device(): jnp.einsum('tpk,tqk->tpq', lax.all_gather(occupied, 'aux', axis=1, tiled=...]
    reshape x2 -> x0, local copies, waits for them, and re-layouts: 31.4 us -> none  [the longest x1 23.6 us: on_device(): (integrals * int_mask[:, None, :]).reshape(aux_rows * slab_width, orbitals)]
    transpose x0 -> x1, other arithmetic: none -> 15.9 us  [on_grid(): ints = jnp.transpose(picked * expand(pattern, BLK)[:, None, :], (1, 0, 2))]
    transpose x0 -> x2, local copies, waits for them, and re-layouts: none -> 15 us  [turned(): return jnp.transpose(v, (0, 2, 3, 1)).reshape(times, slab * cols, aux_rows)]
    mul x2 -> x1, other arithmetic: 14.5 us -> 1.89 us  [on_grid(): masked_density = density * expand(dens_pattern, BLK)[None]]
  transfers between devices with their start and end apart: 4 -> 3, of which waited for: 2 -> 1; matrix products, arithmetic and copies ran while one was open for 15% -> 16% of each run, Pallas kernels for 0% -> 0%
where the time goes in v1:
time: 288 us; the launch traced here: 287 us
  Pallas kernels  183 us (64%)
  waiting for transfers between devices  37.7 us (13%)
  local copies, waits for them, and re-layouts  33.2 us (12%)
  other arithmetic  19.1 us (7%)
  between operations  13.4 us (5%)
    pallas_call x1, Pallas kernels, on_grid(): pl.pallas_call(functools.partial(ring_kernel, CHUNKS), out_shape=jax.Shap...  183 us
    all_gather x1, waiting for transfers between devices, on_grid(): d_own = lax.all_gather(masked_density, 'aux', axis=1, tiled=True)  37.6 us
    transpose x1, other arithmetic, on_grid(): ints = jnp.transpose(picked * expand(pattern, BLK)[:, None, :], (1, 0, 2))  15.9 us
    transpose x2, local copies, waits for them, and re-layouts, turned(): return jnp.transpose(v, (0, 2, 3, 1)).reshape(times, slab * cols, aux_rows)  15 us
    dynamic_slice x1, local copies, waits for them, and re-layouts, on_grid(): picked = lax.dynamic_slice_in_dim(integrals, core * mine, mine, 0)  8.36 us
  transfers between devices with their start and end apart: 3, of which 1 were waited for; matrix products, arithmetic and copies ran while one was open for 16% of the time, Pallas kernels for 0%

profile of v1, /device:TPU:0, one launch (start us, length us, event | category | flops | bytes accessed | tf_op | source)
XLA Modules:
  0.0 287.0 jit_solution(16392804990571445452)
XLA Ops:
  6.5 0.0 all-gather.2.cloned.1.call-start
  6.5 0.7 convert_element_type.33
  7.2 0.1 broadcast_in_dim.16
  7.3 0.1 convert_element_type.34
  7.4 0.1 copy.13
  7.6 1.9 broadcast_multiply_fusion
  9.4 0.0 all-gather.2.cloned.1.call-update
  9.5 0.5 collective-permute-start.1
  10.0 37.6 %all-gather.2.cloned.1.call-done.d_own = bf16[2,2048,256]{2,1,0:T(8,128)(2,1)} async-done(((bf16[2,512,256]{2,1,0:T(8,128)(2,1)}), bf16[2,2048,256]{2,1,0:T(8,128)(2,1)}) %all-gather.2.cloned.1.call-update) | async-done | bytes 2097168 | tf_op jit(solution)/shard_map/all_gather | solution.py:210
  47.6 0.0 collective-permute-start
  47.6 0.7 dynamic-slice_convert_fusion
  48.3 0.1 copy.11
  48.4 0.1 broadcast_in_dim.14
  48.5 0.1 convert_element_type.31
  48.6 1.5 broadcast_in_dim.15
  50.1 2.9 %copy.12 = bf16[512,2048]{1,0:T(8,128)(2,1)S(1)} copy(bf16[512,2048]{0,1:T(8,128)(2,1)} %bitcast.12) | data formatting | bytes 4194304 | tf_op jit(solution)/shard_map/convert_element_type | solution.py:16
  53.1 7.4 %copy.14 = bf16[2,4,256,1024]{3,2,1,0:T(8,128)(2,1)} copy(bf16[2,4,256,1024]{2,1,3,0:T(4,128)(2,1)} %bitcast.13) | data formatting | bytes 8388608 | tf_op jit(solution)/shard_map/transpose | solution.py:217
  60.5 8.4 %constant_dynamic-slice_fusion = bf16[512,4,2048]{2,1,0:T(4,128)(2,1)} fusion(bf16[1024,4,2048]{2,1,0:T(4,128)(2,1)} %param.5, s32[]{:T(128)S(6)} %select_n.14), kind=kLoop, calls=%fused_computation.4 | loop fusion | bytes 16777220 | tf_op jit(solution)/shard_map/dynamic_slice | solution.py:212
  68.9 15.9 %fusion.ints = bf16[4,512,2048]{2,1,0:T(8,128)(2,1)} fusion(bf16[512,4,2048]{2,1,0:T(4,128)(2,1)} %constant_dynamic-slice_fusion, bf16[512,2048]{1,0:T(8,128)(2,1)S(1)} %copy.12), kind=kLoop, calls=%fused_computation.1 | loop fusion | flops 4194304 | bytes 18874368 | tf_op jit(solution)/shard_map/transpose | solution.py:214
  84.7 0.0 collective-permute-done.1
  84.7 7.5 %copy.15 = bf16[2,4,256,1024]{3,2,1,0:T(8,128)(2,1)} copy(bf16[2,4,256,1024]{2,1,3,0:T(4,128)(2,1)} %bitcast.5) | data formatting | bytes 8388608 | tf_op jit(solution)/shard_map/transpose | solution.py:217
  92.3 0.0 collective-permute-done.d_sib
  92.3 183.0 %shard_map.55 = f32[2,512,1024]{2,1,0:T(8,128)} custom-call(bf16[4,512,2048]{2,1,0:T(8,128)(2,1)} %fusion.ints, bf16[2,2048,256]{2,1,0:T(8,128)(2,1)} %all-gather.2.cloned.1.call-done.d_own, bf16[2,2048,256]{2,1,0:T(8,128)(2,1)} %collective-permute-done.d_sib, bf16[2,1024,1024]{2,1,0:T(8,128)(2,1)} %bitcast.14, bf16[2,1024,1024]{2,1,0:T(8,128)(2,1)} %bitcast.15), custom_call_target="tpu_custom_call" | custom-call | flops 25769803776 | bytes 67108864 | tf_op jit(solution)/shard_map/pallas_call | solution.py:223
  275.3 4.8 %copy.21 = f32[2,512,1024]{2,1,0:T(8,128)} copy(f32[2,512,1024]{2,1,0:T(8,128)} %shard_map.55) | data formatting | bytes 8388608
  (1 shorter events, 0.0 us)
Async XLA Ops:
  6.5 41.1 %all-gather.2.cloned.1.call-start = ((), (), s32[]{:S(2)}) async-start(), calls=%async_computation | async-start | bytes 2621440 | tf_op jit(solution)/shard_map/all_gather | solution.py:210
  9.5 75.3 %collective-permute-start.1 = (bf16[2,1024,4,256]{3,2,1,0:T(4,128)(2,1)}, bf16[2,1024,4,256]{3,2,1,0:T(4,128)(2,1)}, u32[]{:S(2)}, u32[]{:S(2)}) collective-permute-start(bf16[2,1024,4,256]{3,2,1,0:T(4,128)(2,1)} %param.9), channel_id=1, source_target_pairs={{0,1},{1,0},{2,3},{3,2},{4,5},{5,4},{6,7},{7,6},{8,9},{9,8},{10,11... | collective-permute-start | bytes 12582920 | tf_op jit(solution)/shard_map/ppermute | solution.py:208
  47.6 44.6 %collective-permute-start = (bf16[2,2048,256]{2,1,0:T(8,128)(2,1)}, bf16[2,2048,256]{2,1,0:T(8,128)(2,1)}, u32[]{:S(2)}, u32[]{:S(2)}) collective-permute-start(bf16[2,2048,256]{2,1,0:T(8,128)(2,1)} %all-gather.2.cloned.1.call-done.d_own), channel_id=1, source_target_pairs={{0,1},{1,0},{2,3},{3,2},{4,5},{5,4},{6,7},{7,6},{8,9},{9,8},{10,11... | collective-permute-start | bytes 6291464 | tf_op jit(solution)/shard_map/ppermute | solution.py:211
Sparse Core Ops, SparseCore 0:
  9.6 38.0 all-gather.1

commit v2 on v1

--- a/solution.py
+++ b/solution.py
@@ -18,10 +18,13 @@
     )
 
 
-def ring_kernel(chunks, ints, d_own, d_sib, v_own, v_sib, out, occ, psum, zrecv, ibuf, isem, xs, xr, zs, zr):
-    slab, rows = ibuf.shape[1], ibuf.shape[2]
+def ring_kernel(
+    chunks, ints, mask, dens, virt, out, occ, psum, zrecv, ibuf, ybuf, dall, vall,
+    isem, xs, xr, zs, zr, dl, ds, dr, es, er, vl, vs, vr,
+):
+    rows, slab = ibuf.shape[1], ibuf.shape[2]
     per_moment = out.shape[1] // rows
-    cols = d_own.shape[2]
+    cols = dens.shape[2]
     width = slab * cols
     half = rows // 2
     a = lax.axis_index("aux")
@@ -30,6 +33,9 @@
     ax = a + 1 - 2 * (a % 2)
     ay = (a + 2) % 4
     ad = 3 - a
+    core = o % 2
+    sib = o + 1 - 2 * core
+    depth = dens.shape[1]
 
     def rcopy(src, dst, send, recv, dev):
         return pltpu.make_async_remote_copy(
@@ -55,14 +61,42 @@
 
     def fetch(i):
         return pltpu.make_async_copy(
-            ints.at[:, pl.ds((i % per_moment) * rows, rows), :], ibuf.at[i % 2], isem.at[i % 2]
+            ints.at[pl.ds(core * out.shape[1] + (i % per_moment) * rows, rows)], ibuf.at[i % 2], isem.at[i % 2]
         )
 
+    def d_local(t):
+        return pltpu.make_async_copy(dens.at[t], dall.at[0, t, a], dl.at[t])
+
+    def d_own(t, kind):
+        return rcopy(
+            dens.at[t], dall.at[0, t, a], ds.at[kind, t], dr.at[kind, t], (ax if kind == 0 else ay, o)
+        )
+
+    def d_forward(t, kind, slot):
+        part = pl.ds(0 if kind == 2 else depth // 2, depth // 2)
+        ref = dall.at[0, t, slot, part]
+        return rcopy(ref, ref, ds.at[kind, t], dr.at[kind, t], (ay if kind == 2 else ax, o))
+
+    def d_cross(t, kind, slot):
+        src = dens.at[t] if kind == 0 else dall.at[0, t, slot]
+        return rcopy(src, dall.at[1, t, slot], es.at[kind, t], er.at[kind, t], (a, sib))
+
+    def v_local(t):
+        return pltpu.make_async_copy(virt.at[t], vall.at[0, t], vl.at[t])
+
+    def v_cross(t):
+        return rcopy(virt.at[t], vall.at[1, t], vs.at[t], vr.at[t], (a, sib))
+
     fetch(0).start()
+    d_local(0).start()
+    v_local(0).start()
+    d_local(1).start()
+    v_local(1).start()
 
     barrier = pltpu.get_barrier_semaphore()
     pl.semaphore_signal(barrier, inc=1, device_id=(ax, o), device_id_type=MESH)
     pl.semaphore_signal(barrier, inc=1, device_id=(ay, o), device_id_type=MESH)
+    pl.semaphore_signal(barrier, inc=1, device_id=(a, sib), device_id_type=MESH)
 
     @pl.when(z > 0)
     def _():
@@ -76,11 +110,37 @@
 
     @pl.when(inner)
     def _():
-        pl.semaphore_wait(barrier, 4)
+        pl.semaphore_wait(barrier, 5)
 
     @pl.when(jnp.logical_not(inner))
     def _():
-        pl.semaphore_wait(barrier, 3)
+        pl.semaphore_wait(barrier, 4)
+
+    def d_send(t):
+        d_own(t, 0).start()
+        d_own(t, 1).start()
+        d_cross(t, 0, a).start()
+        v_cross(t).start()
+
+    def d_relay(t):
+        d_own(t, 0).wait_recv()
+        d_forward(t, 2, ax).start()
+        d_cross(t, 1, ax).start()
+        d_own(t, 1).wait_recv()
+        d_forward(t, 3, ay).start()
+        d_cross(t, 2, ay).start()
+
+    def d_finish(t):
+        d_forward(t, 2, ad).wait_recv()
+        d_forward(t, 3, ad).wait_recv()
+        d_cross(t, 3, ad).start()
+        d_local(t).wait()
+        for kind, slot in enumerate((a, ax, ay, ad)):
+            d_cross(t, kind, slot).wait_recv()
+
+    d_send(0)
+    d_relay(0)
+    d_finish(0)
 
     def make(i):
         fetch(i).wait()
@@ -90,11 +150,18 @@
             fetch(i + 1).start()
 
         t = i // per_moment
-        x = ibuf[i % 2].reshape(slab * rows, ibuf.shape[3])
-        for base, dens in ((0, d_own), (width, d_sib)):
-            y = jnp.dot(x, dens[t], preferred_element_type=jnp.float32).astype(jnp.bfloat16)
+        x = (ibuf[i % 2] * mask[i % per_moment][None]).reshape(rows * slab, ibuf.shape[3])
+        for side in range(2):
+            d = dall[side, t].reshape(4 * depth, cols)
+            y = jnp.dot(x, d, preferred_element_type=jnp.float32)
+            for part in range(cols // 128):
+                ybuf[part] = y[:, part * 128 : (part + 1) * 128]
             for s in range(slab):
-                occ[a, i, :, base + s * cols : base + (s + 1) * cols] = y[s * rows : (s + 1) * rows]
+                base = side * width + s * cols
+                for part in range(cols // 128):
+                    piece = ybuf[part, pl.ds(s, rows, stride=slab), :]
+                    low = base + part * 128
+                    occ[a, i, :, low : low + 128] = piece.astype(jnp.bfloat16)
         own(i, 0, a).start()
         own(i, 1, a).start()
 
@@ -108,10 +175,16 @@
         forward(i, 2, ad).wait_recv()
         forward(i, 3, ad).wait_recv()
         t = i // per_moment
+
+        @pl.when(i % per_moment == 0)
+        def _():
+            v_local(t).wait()
+            v_cross(t).wait_recv()
+
         for d in range(0, 4, 2):
             left = occ[d : d + 2, i].reshape(2 * rows, 2 * width)
-            p = jnp.dot(left[:, :width], v_own[t], preferred_element_type=jnp.float32)
-            p += jnp.dot(left[:, width:], v_sib[t], preferred_element_type=jnp.float32)
+            p = jnp.dot(left[:, :width], vall[0, t], preferred_element_type=jnp.float32)
+            p += jnp.dot(left[:, width:], vall[1, t], preferred_element_type=jnp.float32)
             psum[i, d : d + 2] = p.astype(jnp.bfloat16).reshape(2, rows, psum.shape[3])
 
         @pl.when(z == 0)
@@ -182,6 +255,21 @@
             @pl.when((step >= lag) & (step < chunks + lag))
             def _(stage=stage, lag=lag):
                 stage(step - lag)
+
+        for at, part in ((1, d_send), (3, d_relay), (5, d_finish)):
+
+            @pl.when(step == at)
+            def _(part=part):
+                part(1)
+
+    for t in range(2):
+        for kind in range(2):
+            d_own(t, kind).wait_send()
+        d_forward(t, 2, ax).wait_send()
+        d_forward(t, 3, ay).wait_send()
+        for kind, slot in enumerate((a, ax, ay, ad)):
+            d_cross(t, kind, slot).wait_send()
+        v_cross(t).wait_send()
 
     @pl.loop(0, chunks)
     def _(i):
@@ -204,37 +292,45 @@
     times, _, cols = density.shape
     core = lax.axis_index("orb") % 2
     mine = aux_rows // 2
-    pairs = [(i, i + 1 - 2 * (i % 2)) for i in range(8)]
-    v_other = lax.ppermute(virt_ints, "orb", pairs)
     masked_density = density * expand(dens_pattern, BLK)[None]
-    d_own = lax.all_gather(masked_density, "aux", axis=1, tiled=True)
-    d_sib = lax.ppermute(d_own, "orb", pairs)
-    picked = lax.dynamic_slice_in_dim(integrals, core * mine, mine, 0)
     pattern = lax.dynamic_slice_in_dim(int_pattern, core * (mine // BLK), mine // BLK, 0)
-    ints = jnp.transpose(picked * expand(pattern, BLK)[:, None, :], (1, 0, 2))
+    rows = times * mine // CHUNKS
+    mask = jnp.repeat(pattern, BLK, axis=1).astype(jnp.bfloat16)
+    mask = jnp.repeat(mask, BLK // rows, axis=0)[:, None, :]
 
     def turned(v):
         return jnp.transpose(v, (0, 2, 3, 1)).reshape(times, slab * cols, aux_rows)
 
-    rows = times * mine // CHUNKS
     width = slab * cols
     bf16 = jnp.bfloat16
+    hbm = pl.BlockSpec(memory_space=pl.ANY)
     vmem = pl.BlockSpec(memory_space=pltpu.VMEM)
     return pl.pallas_call(
         functools.partial(ring_kernel, CHUNKS),
         out_shape=jax.ShapeDtypeStruct((times, mine, aux_rows), jnp.float32),
-        in_specs=[pl.BlockSpec(memory_space=pl.ANY), vmem, vmem, vmem, vmem],
+        in_specs=[hbm, vmem, vmem, hbm],
         out_specs=vmem,
         scratch_shapes=[
             pltpu.VMEM((4, CHUNKS, rows, 2 * width), bf16),
             pltpu.VMEM((CHUNKS, 4, rows, aux_rows), bf16),
             pltpu.VMEM((CHUNKS, 5, rows, aux_rows), bf16),
-            pltpu.VMEM((2, slab, rows, orbitals), bf16),
+            pltpu.VMEM((2, rows, slab, orbitals), bf16),
+            pltpu.VMEM((cols // 128, rows * slab, 128), jnp.float32),
+            pltpu.VMEM((2, times, 4, orbitals // 4, cols), bf16),
+            pltpu.VMEM((2, times, width, aux_rows), bf16),
             pltpu.SemaphoreType.DMA((2,)),
             pltpu.SemaphoreType.DMA((4, CHUNKS)),
             pltpu.SemaphoreType.DMA((4, CHUNKS)),
             pltpu.SemaphoreType.DMA((2, CHUNKS)),
             pltpu.SemaphoreType.DMA((2, CHUNKS)),
+            pltpu.SemaphoreType.DMA((2,)),
+            pltpu.SemaphoreType.DMA((4, 2)),
+            pltpu.SemaphoreType.DMA((4, 2)),
+            pltpu.SemaphoreType.DMA((4, 2)),
+            pltpu.SemaphoreType.DMA((4, 2)),
+            pltpu.SemaphoreType.DMA((2,)),
+            pltpu.SemaphoreType.DMA((2,)),
+            pltpu.SemaphoreType.DMA((2,)),
         ],
         compiler_params=pltpu.CompilerParams(
             collective_id=0, has_side_effects=True, vmem_limit_bytes=60 * 1024 * 1024
@@ -244,7 +340,7 @@
             bytes_accessed=64 << 20,
             transcendentals=0,
         ),
-    )(ints, d_own, d_sib, turned(virt_ints), turned(v_other))
+    )(integrals, mask, masked_density, turned(virt_ints))
 
 
 def on_device(integrals, int_pattern, density, dens_pattern, virt_ints):

time: 288 us -> 220 us (0.76)
  waiting for transfers between devices: 37.7 us -> 0 us
  Pallas kernels: 183 us -> 203 us
  local copies, waits for them, and re-layouts: 33.2 us -> 13.3 us
  other arithmetic: 19.1 us -> 3.26 us
  between operations: 13.4 us -> 0.03 us
    all_gather x1 -> x0, waiting for transfers between devices: 37.6 us -> none  [on_grid(): d_own = lax.all_gather(masked_density, 'aux', axis=1, tiled=True)]
    pallas_call x1, Pallas kernels: 183 us -> 203 us  [on_grid(): pl.pallas_call(functools.partial(ring_kernel, CHUNKS), out_shape=jax.Shap...]
    transpose x1 -> x0, other arithmetic: 15.9 us -> none  [on_grid(): ints = jnp.transpose(picked * expand(pattern, BLK)[:, None, :], (1, 0, 2))]
    dynamic_slice x1 -> x0, local copies, waits for them, and re-layouts: 8.36 us -> none  [on_grid(): picked = lax.dynamic_slice_in_dim(integrals, core * mine, mine, 0)]
    transpose x2 -> x1, local copies, waits for them, and re-layouts: 15 us -> 7.43 us  [turned(): return jnp.transpose(v, (0, 2, 3, 1)).reshape(times, slab * cols, aux_rows)]
    convert_element_type x5 -> x2, local copies, waits for them, and re-layouts: 3.36 us -> 0.22 us  [expand(): jnp.repeat(jnp.repeat(pattern, block_width, axis=0), block_width, axis=1)]
  transfers between devices with their start and end apart: 3 -> 0, of which waited for: 1 -> 0; matrix products, arithmetic and copies ran while one was open for 16% -> 0% of each run, Pallas kernels for 0% -> 0%
where the time goes in v2:
time: 220 us; the launch traced here: 219 us
  Pallas kernels  203 us (92%)
  local copies, waits for them, and re-layouts  13.3 us (6%)
  other arithmetic  3.26 us (1%)
    pallas_call x1, Pallas kernels, on_grid(): pl.pallas_call(functools.partial(ring_kernel, CHUNKS), out_shape=jax.Shap...  203 us
    transpose x1, local copies, waits for them, and re-layouts, turned(): return jnp.transpose(v, (0, 2, 3, 1)).reshape(times, slab * cols, aux_rows)  7.43 us
    unnamed x1, local copies, waits for them, and re-layouts  4.79 us

profile of v2, /device:TPU:0, one launch (start us, length us, event | category | flops | bytes accessed | tf_op | source)
XLA Modules:
  0.0 219.3 jit_solution(15226412084312903310)
XLA Ops:
  0.0 0.7 convert_element_type.31
  0.7 0.7 dynamic-slice_convert_fusion
  1.4 0.1 broadcast_in_dim.12
  1.4 0.1 convert_element_type.32
  1.5 0.1 broadcast_in_dim.11
  1.6 0.7 convert_element_type.34.mask
  2.4 0.1 copy.8
  2.5 1.9 broadcast_multiply_fusion.dens
  4.4 7.4 %copy.9 = bf16[2,4,256,1024]{3,2,1,0:T(8,128)(2,1)} copy(bf16[2,4,256,1024]{2,1,3,0:T(4,128)(2,1)} %bitcast.5) | data formatting | bytes 8388608 | tf_op jit(solution)/shard_map/transpose | solution.py:302
  11.8 202.7 %shard_map.55 = f32[2,512,1024]{2,1,0:T(8,128)} custom-call(bf16[1024,4,2048]{2,1,0:T(4,128)(2,1)} %ints.1, bf16[8,1,2048]{2,1,0:T(2,128)(2,1)} %convert_element_type.34.mask, bf16[2,512,256]{2,1,0:T(8,128)(2,1)} %broadcast_multiply_fusion.dens, bf16[2,1024,1024]{2,1,0:T(8,128)(2,1)} %bitcast.6), custom_call_target="tpu_custom_call" | custom-call | flops 25769803776 | bytes 67108864 | tf_op jit(solution)/shard_map/pallas_call | solution.py:308
  214.5 4.8 %copy.12 = f32[2,512,1024]{2,1,0:T(8,128)} copy(f32[2,512,1024]{2,1,0:T(8,128)} %shard_map.55) | data formatting | bytes 8388608
  (1 shorter events, 0.0 us)

commit v3 on v2

--- a/solution.py
+++ b/solution.py
@@ -8,7 +8,7 @@
 from jax.sharding import PartitionSpec as P
 
 BLK = 64
-CHUNKS = 16
+CHUNKS = 32
 MESH = pl.DeviceIdType.MESH
 
 
@@ -246,7 +246,7 @@
             total = zrecv[i, z].astype(jnp.float32) + zrecv[i, z + 1].astype(jnp.float32)
             out[t, where] = total + psum[i, z].astype(jnp.float32)
 
-    stages = ((make, 0), (relay, 2), (multiply, 3), (hop1, 4), (hop2, 5), (finish, 6))
+    stages = ((relay, 2), (make, 0), (multiply, 4), (hop1, 6), (hop2, 8), (finish, 10))
 
     @pl.loop(0, chunks + stages[-1][1])
     def _(step):

time: 220 us -> 209 us (0.950)
  Pallas kernels: 203 us -> 191 us
    pallas_call x1, Pallas kernels: 203 us -> 191 us  [on_grid(): pl.pallas_call(functools.partial(ring_kernel, CHUNKS), out_shape=jax.Shap...]
where the time goes in v3:
time: 209 us; the launch traced here: 208 us
  Pallas kernels  191 us (91%)
  local copies, waits for them, and re-layouts  13.5 us (6%)
  other arithmetic  3.26 us (2%)
    pallas_call x1, Pallas kernels, on_grid(): pl.pallas_call(functools.partial(ring_kernel, CHUNKS), out_shape=jax.Shap...  191 us
    transpose x1, local copies, waits for them, and re-layouts, turned(): return jnp.transpose(v, (0, 2, 3, 1)).reshape(times, slab * cols, aux_rows)  7.43 us
    unnamed x1, local copies, waits for them, and re-layouts  4.79 us

profile of v3, /device:TPU:0, one launch (start us, length us, event | category | flops | bytes accessed | tf_op | source)
XLA Modules:
  0.0 208.3 jit_solution(7867072731546546922)
XLA Ops:
  0.0 0.7 convert_element_type.24
  0.7 0.7 dynamic-slice_convert_fusion
  1.4 0.1 broadcast_in_dim.15
  1.4 0.1 convert_element_type.25
  1.5 0.1 broadcast_in_dim.13
  1.6 0.1 convert_element_type.23
  1.8 0.7 broadcast_in_dim_reshape.4.mask
  2.6 0.1 copy.8
  2.7 1.9 broadcast_multiply_fusion.dens
  4.6 7.4 %copy.9 = bf16[2,4,256,1024]{3,2,1,0:T(8,128)(2,1)} copy(bf16[2,4,256,1024]{2,1,3,0:T(4,128)(2,1)} %bitcast.5) | data formatting | bytes 8388608 | tf_op jit(solution)/shard_map/transpose | solution.py:302
  12.0 191.5 %shard_map.55 = f32[2,512,1024]{2,1,0:T(8,128)} custom-call(bf16[1024,4,2048]{2,1,0:T(4,128)(2,1)} %ints.1, bf16[16,1,2048]{2,1,0:T(2,128)(2,1)} %broadcast_in_dim_reshape.4.mask, bf16[2,512,256]{2,1,0:T(8,128)(2,1)} %broadcast_multiply_fusion.dens, bf16[2,1024,1024]{2,1,0:T(8,128)(2,1)} %bitcast.6), custom_call_target="tpu_custom_call" | custom-call | flops 25769803776 | bytes 67108864 | tf_op jit(solution)/shard_map/pallas_call | solution.py:308
  203.5 4.8 %copy.12 = f32[2,512,1024]{2,1,0:T(8,128)} copy(f32[2,512,1024]{2,1,0:T(8,128)} %shard_map.55) | data formatting | bytes 8388608
  (2 shorter events, 0.1 us)

commit v4 on v3

--- a/solution.py
+++ b/solution.py
@@ -20,7 +20,7 @@
 
 def ring_kernel(
     chunks, ints, mask, dens, virt, out, occ, psum, zrecv, ibuf, ybuf, dall, vall,
-    isem, xs, xr, zs, zr, dl, ds, dr, es, er, vl, vs, vr,
+    isem, xs, xr, zs, zr, dl, ds, dr, es, er, vl, vs, vr, obuf, osem,
 ):
     rows, slab = ibuf.shape[1], ibuf.shape[2]
     per_moment = out.shape[1] // rows
@@ -227,24 +227,31 @@
             add(i, 0, 0)
             down(i, 1, False).start()
 
+    def flush(i):
+        where = pl.ds((i % per_moment) * rows, rows)
+        return pltpu.make_async_copy(obuf.at[i % 2], out.at[i // per_moment, where], osem.at[i % 2])
+
     def finish(i):
-        where = pl.ds((i % per_moment) * rows, rows)
-        t = i // per_moment
+        @pl.when(i >= 2)
+        def _():
+            flush(i - 2).wait()
 
         @pl.when(z == 0)
         def _():
             down(i, 1, False).wait_recv()
-            out[t, where] = psum[i, 0].astype(jnp.float32) + zrecv[i, 0].astype(jnp.float32)
+            obuf[i % 2] = psum[i, 0].astype(jnp.float32) + zrecv[i, 0].astype(jnp.float32)
 
         @pl.when(z == 3)
         def _():
             up(i, 2, False).wait_recv()
-            out[t, where] = psum[i, 3].astype(jnp.float32) + zrecv[i, 4].astype(jnp.float32)
+            obuf[i % 2] = psum[i, 3].astype(jnp.float32) + zrecv[i, 4].astype(jnp.float32)
 
         @pl.when(inner)
         def _():
             total = zrecv[i, z].astype(jnp.float32) + zrecv[i, z + 1].astype(jnp.float32)
-            out[t, where] = total + psum[i, z].astype(jnp.float32)
+            obuf[i % 2] = total + psum[i, z].astype(jnp.float32)
+
+        flush(i).start()
 
     stages = ((relay, 2), (make, 0), (multiply, 4), (hop1, 6), (hop2, 8), (finish, 10))
 
@@ -262,6 +269,8 @@
             def _(part=part):
                 part(1)
 
+    flush(chunks - 2).wait()
+    flush(chunks - 1).wait()
     for t in range(2):
         for kind in range(2):
             d_own(t, kind).wait_send()
@@ -309,7 +318,7 @@
         functools.partial(ring_kernel, CHUNKS),
         out_shape=jax.ShapeDtypeStruct((times, mine, aux_rows), jnp.float32),
         in_specs=[hbm, vmem, vmem, hbm],
-        out_specs=vmem,
+        out_specs=hbm,
         scratch_shapes=[
             pltpu.VMEM((4, CHUNKS, rows, 2 * width), bf16),
             pltpu.VMEM((CHUNKS, 4, rows, aux_rows), bf16),
@@ -330,6 +339,8 @@
             pltpu.SemaphoreType.DMA((4, 2)),
             pltpu.SemaphoreType.DMA((2,)),
             pltpu.SemaphoreType.DMA((2,)),
+            pltpu.SemaphoreType.DMA((2,)),
+            pltpu.VMEM((2, rows, aux_rows), jnp.float32),
             pltpu.SemaphoreType.DMA((2,)),
         ],
         compiler_params=pltpu.CompilerParams(

time: 209 us -> 207 us (level)
  no operation moved by 1% of the time
where the time goes in v4:
time: 207 us
  Pallas kernels  190 us (92%)
  local copies, waits for them, and re-layouts  13.5 us (7%)
  other arithmetic  3.26 us (2%)
    pallas_call x1, Pallas kernels, on_grid(): pl.pallas_call(functools.partial(ring_kernel, CHUNKS), out_shape=jax.Shap...  190 us
    transpose x1, local copies, waits for them, and re-layouts, turned(): return jnp.transpose(v, (0, 2, 3, 1)).reshape(times, slab * cols, aux_rows)  7.43 us
    unnamed x1, local copies, waits for them, and re-layouts  4.79 us

profile of v4, /device:TPU:0, one launch (start us, length us, event | category | flops | bytes accessed | tf_op | source)
XLA Modules:
  0.0 207.0 jit_solution(7027042005845796879)
XLA Ops:
  0.0 0.7 convert_element_type.24
  0.7 0.7 dynamic-slice_convert_fusion
  1.4 0.1 broadcast_in_dim.15
  1.4 0.1 convert_element_type.25
  1.5 0.1 broadcast_in_dim.13
  1.6 0.1 convert_element_type.23
  1.8 0.7 broadcast_in_dim_reshape.4.mask
  2.6 0.1 copy.8
  2.7 1.9 broadcast_multiply_fusion.dens
  4.6 7.4 %copy.9 = bf16[2,4,256,1024]{3,2,1,0:T(8,128)(2,1)} copy(bf16[2,4,256,1024]{2,1,3,0:T(4,128)(2,1)} %bitcast.5) | data formatting | bytes 8388608 | tf_op jit(solution)/shard_map/transpose | solution.py:311
  12.0 190.1 %shard_map.55 = f32[2,512,1024]{2,1,0:T(8,128)} custom-call(bf16[1024,4,2048]{2,1,0:T(4,128)(2,1)} %ints.1, bf16[16,1,2048]{2,1,0:T(2,128)(2,1)} %broadcast_in_dim_reshape.4.mask, bf16[2,512,256]{2,1,0:T(8,128)(2,1)} %broadcast_multiply_fusion.dens, bf16[2,1024,1024]{2,1,0:T(8,128)(2,1)} %bitcast.6), custom_call_target="tpu_custom_call" | custom-call | flops 25769803776 | bytes 67108864 | tf_op jit(solution)/shard_map/pallas_call | solution.py:317
  202.2 4.8 %copy.12 = f32[2,512,1024]{2,1,0:T(8,128)} copy(f32[2,512,1024]{2,1,0:T(8,128)} %shard_map.55) | data formatting | bytes 8388608
  (2 shorter events, 0.1 us)
